TPU v7x, 768 devices: a whole 4x8x12 slice. The times are simulated.
768 devices in a mesh: dp: 12 (over z), table: 64 (over y, x, core).
Axes of the slice: x: 4, y: 8, z: 12, core: 2. Of those that a mesh axis runs over, the one named last changes fastest.
Arguments:
- item_ids: int32 [196608], P(('dp', 'table')), may hold values from 0 to 65535, as said below
- lengths: int32 [768, 4], P(('dp', 'table')), may hold values from 1 to 128, 256 in all within a row
- item_table: bfloat16 [65536, 1024], P('table'), may hold values from -6 to 6
- admitted: int32 [65536], P('table'), may hold values 0 or 1
- input_weight: bfloat16 [1024, 2048], replicated, may hold values from -0.1875 to 0.1875
- output_weight: bfloat16 [512, 1024], replicated, may hold values from -0.25 to 0.25
- out_grad: bfloat16 [196608, 1024], P(('dp', 'table')), may hold values from -6 to 6
Outputs:
- layer_out: bfloat16 [196608, 1024], P(('dp', 'table'))
- embed_grad: float32 [196608, 1024], P(('dp', 'table'))
- weight_grad: float32 [512, 1024], P('table')
Inputs may be any that keep to these rules, and one draw needn't show every extreme that they name: `item_ids`: in each aligned block of 256 ids, at most 8 lie in one table shard (ids k * 1024 to (k + 1) * 1024 - 1); in each group of 64 consecutive blocks one shard receives exactly 8 ids from every block of the group. The 4 lengths of a device sum to 256.
All inputs are finite; a program needn't handle non-finite values. No bound on the sum of `admitted` on one device may be relied on, other than what follows from the above.
Results may differ from a plain program's by a relative error of at most 0.0085.
Values may be sent and summed in bfloat16 or wider, within the bound.
A program may use at most 64 MiB of HBM per device.

v0:
```python
import math

import jax
import jax.numpy as jnp
from jax import lax
from jax.sharding import PartitionSpec as P

HEADS = 4
MOST = 128


epsilon = 1e-05


def silu_slope(argument):
    logistic = jax.nn.sigmoid(argument)
    return logistic * (1.0 + argument * (1.0 - logistic))


def layer_norm(inputs):
    centre = inputs - jnp.mean(inputs, -1, keepdims=True)
    inverse = lax.rsqrt(jnp.mean(centre * centre, -1, keepdims=True) + epsilon)
    return (centre * inverse, inverse)


def norm_back(upstream, normed, inverse):
    return inverse * (
        upstream
        - jnp.mean(upstream, -1, keepdims=True)
        - normed * jnp.mean(upstream * normed, -1, keepdims=True)
    )


def contract(pattern, left_side, right_side):
    return jnp.einsum(pattern, left_side, right_side, preferred_element_type=jnp.float32)


def contract_first(left_side, right_side):
    return lax.dot_general(
        left_side, right_side, (((0,), (0,)), ((), ())), preferred_element_type=jnp.float32
    )


def contract_last(left_side, right_side):
    return lax.dot_general(
        left_side, right_side, (((1,), (1,)), ((), ())), preferred_element_type=jnp.float32
    )


def local_layer(fetched, admit_flags, out_grad, seq_lengths, input_weight, output_weight):
    token_count = fetched.shape[0]
    feature_width = output_weight.shape[0]
    head_size = feature_width // HEADS
    positions = jnp.arange(token_count, dtype=jnp.int32)
    seq_ends = jnp.cumsum(seq_lengths)
    segment = jnp.sum((positions[:, None] >= seq_ends[None, :]).astype(jnp.int32), axis=1)
    visible = (segment[:, None] == segment[None, :]) & (positions[None, :] <= positions[:, None])
    fetched_wide = fetched.astype(jnp.float32)
    normed, input_scale = layer_norm(fetched_wide)
    projected = jnp.dot(
        normed.astype(jnp.bfloat16), input_weight, preferred_element_type=jnp.float32
    )
    activated = jax.nn.silu(projected).astype(jnp.bfloat16)
    gating = activated[:, :feature_width]
    values = activated[:, feature_width : 2 * feature_width].reshape(token_count, HEADS, head_size)
    queries = activated[:, 2 * feature_width : 3 * feature_width].reshape(
        token_count, HEADS, head_size
    )
    keys_part = activated[:, 3 * feature_width :].reshape(token_count, HEADS, head_size)
    scores = contract("ihd,jhd->hij", queries, keys_part)
    weights = jnp.where(visible[None], jax.nn.silu(scores) / MOST, 0.0).astype(jnp.bfloat16)
    attended = contract("hij,jhd->ihd", weights, values).reshape(token_count, feature_width)
    head_norm, head_scale = layer_norm(attended)
    mixed_out = (head_norm * gating.astype(jnp.float32)).astype(jnp.bfloat16)
    layer_out = (
        fetched_wide + jnp.dot(mixed_out, output_weight, preferred_element_type=jnp.float32)
    ).astype(jnp.bfloat16)
    weight_term = contract_first(mixed_out, out_grad)
    grad_mixed = contract_last(out_grad, output_weight)
    grad_attended = norm_back(
        grad_mixed * gating.astype(jnp.float32), head_norm, head_scale
    ).astype(jnp.bfloat16)
    grad_attended = grad_attended.reshape(token_count, HEADS, head_size)
    grad_weights = contract("ihd,jhd->hij", grad_attended, values)
    grad_values = contract("hij,ihd->jhd", weights, grad_attended).reshape(
        token_count, feature_width
    )
    grad_scores = jnp.where(visible[None], grad_weights * silu_slope(scores) / MOST, 0.0).astype(
        jnp.bfloat16
    )
    grad_queries = contract("hij,jhd->ihd", grad_scores, keys_part).reshape(
        token_count, feature_width
    )
    grad_keys = contract("hij,ihd->jhd", grad_scores, queries).reshape(token_count, feature_width)
    grad_projected = jnp.concatenate(
        [grad_mixed * head_norm, grad_values, grad_queries, grad_keys], axis=1
    )
    grad_projected = (grad_projected * silu_slope(projected)).astype(jnp.bfloat16)
    grad_normed = contract_last(grad_projected, input_weight)
    embed_grad = admit_flags[:, None] * (
        norm_back(grad_normed, normed, input_scale) + out_grad.astype(jnp.float32)
    )
    return (layer_out, embed_grad, weight_term)


def on_device(item_ids, lengths, item_table, admitted, input_weight, output_weight, out_grad):
    shards = lax.axis_size("table")
    shard_rows = item_table.shape[0]
    token_count = item_ids.shape[0]
    features = item_table.shape[1]
    capacity = max(2, 2 * token_count // shards)
    owner_shard = item_ids // shard_rows
    row_local = item_ids % shard_rows
    onehot = (owner_shard[:, None] == jnp.arange(shards, dtype=jnp.int32)[None, :]).astype(
        jnp.int32
    )
    slot_rank = jnp.sum(jnp.cumsum(onehot, axis=0) * onehot, axis=1) - 1
    outgoing = jnp.zeros((shards, capacity), jnp.int32).at[owner_shard, slot_rank].set(row_local)
    wanted = lax.all_to_all(outgoing, "table", split_axis=0, concat_axis=0, tiled=True)
    looked_up = item_table[wanted]
    looked_flags = admitted[wanted].astype(jnp.bfloat16)
    arrived = lax.all_to_all(looked_up, "table", split_axis=0, concat_axis=0, tiled=True)
    arrived_flags = lax.all_to_all(looked_flags, "table", split_axis=0, concat_axis=0, tiled=True)
    slot_index = owner_shard * capacity + slot_rank
    admit_bf = arrived_flags.reshape(-1)[slot_index]
    fetched = arrived.reshape(-1, features)[slot_index] * admit_bf[:, None]
    layer_out, embed_grad, weight_term = local_layer(
        fetched, admit_bf.astype(jnp.float32), out_grad, lengths[0], input_weight, output_weight
    )
    factor = 1.0 / math.sqrt(token_count * lax.axis_size("dp") * shards)
    scaled = weight_term * factor
    summed = lax.psum(scaled, "dp")
    weight_grad = lax.psum_scatter(summed, "table", scatter_dimension=0, tiled=True)
    return (layer_out, embed_grad, weight_grad)


def solution(mesh):
    return jax.shard_map(
        on_device,
        mesh=mesh,
        in_specs=(
            P(("dp", "table")),
            P(("dp", "table"), None),
            P("table", None),
            P("table"),
            P(),
            P(),
            P(("dp", "table"), None),
        ),
        out_specs=(P(("dp", "table"), None), P(("dp", "table"), None), P("table", None)),
        check_vma=False,
    )
```

profile of v0, /device:TPU:2, one launch (start us, length us, event | category | flops | bytes accessed | tf_op | source)
XLA Modules:
  0.0 387.3 jit_solution(1926299358561995500)
XLA Ops:
  7.2 0.8 compare_select_fusion.3
  9.0 11.3 %scatter_fusion = s32[64,8]{0,1:T(8,128)S(1)} fusion(s32[64,8]{0,1:T(8,128)S(1)} %broadcast.191, s32[256]{0:T(256)S(1)} %bitcast.82, s32[256]{0:T(256)S(1)} %get-tuple-element.18), kind=kCustom, calls=%fused_computation.4 | custom fusion | bytes 5120 | tf_op jit(solution)/shard_map/scatter | solution.py:118
  20.5 21.5 %all_to_all.23 = s32[64,1,8]{2,1,0:T(1,128)S(1)} all-to-all(s32[64,1,8]{2,1,0:T(1,128)S(1)} %copy.52), channel_id=1, replica_groups=mesh['dp'=12,'table'=64] {'table'}, dimensions={0} | all-to-all | bytes 4096 | tf_op jit(solution)/shard_map/all_to_all | solution.py:119
  42.0 2.3 gather_fusion.2
  45.1 5.5 %all-to-all-start.2 = ((bf16[64,1,8]{2,1,0:T(2,128)(2,1)}), bf16[64,1,8]{2,1,0:T(2,128)(2,1)S(1)}, u32[]{:S(2)}, u32[]{:S(2)}) async-start(bf16[64,1,8]{2,1,0:T(2,128)(2,1)} %convert_element_type.79), calls=%async_computation.2 | async-start | bytes 65536 | tf_op jit(solution)/shard_map/all_to_all | solution.py:123
  50.6 2.8 gather_fusion
  53.4 5.8 %all-to-all-done.2 = bf16[64,1,8]{2,1,0:T(2,128)(2,1)S(1)} async-done(((bf16[64,1,8]{2,1,0:T(2,128)(2,1)}), bf16[64,1,8]{2,1,0:T(2,128)(2,1)S(1)}, u32[]{:S(2)}, u32[]{:S(2)}) %all-to-all-start.2) | async-done | bytes 1056 | tf_op jit(solution)/shard_map/all_to_all | solution.py:123
  59.2 5.6 %all-to-all-start.1 = ((bf16[64,8,1024]{2,1,0:T(8,128)(2,1)}), bf16[64,8,1024]{2,1,0:T(8,128)(2,1)S(1)}, u32[]{:S(2)}, u32[]{:S(2)}) async-start(bf16[64,8,1024]{2,1,0:T(8,128)(2,1)} %bitcast.84), calls=%async_computation.1 | async-start | bytes 2097152 | tf_op jit(solution)/shard_map/all_to_all | solution.py:122
  65.2 1.3 dynamic-slice
  67.5 1.9 gather_fusion.3
  69.5 24.2 %all-to-all-done.1 = bf16[64,8,1024]{2,1,0:T(8,128)(2,1)S(1)} async-done(((bf16[64,8,1024]{2,1,0:T(8,128)(2,1)}), bf16[64,8,1024]{2,1,0:T(8,128)(2,1)S(1)}, u32[]{:S(2)}, u32[]{:S(2)}) %all-to-all-start.1) | async-done | bytes 1048608 | tf_op jit(solution)/shard_map/all_to_all | solution.py:122
  93.6 2.0 gather_fusion.1
  95.6 1.3 convert_reduce_fusion
  96.9 1.4 fusion.15
  98.3 5.1 %multiply_convert_fusion = (bf16[256,2048]{1,0:T(8,128)(2,1)S(1)}, f32[256,2048]{1,0:T(8,128)}) fusion(bf16[1024,2048]{1,0:T(8,128)(2,1)} %param.11, f32[256]{0:T(256)S(1)} %add_rsqrt_fusion.1, f32[256]{0:T(256)S(1)} %broadcast_multiply_fusion.6, bf16[256,1024]{1,0:T(8,128)(2,1)} %gather_fusion.1, bf16[256]{0:T(256)(128)(2,1)S(1)} %gather_fusion.3), kind=kOutput, calls=%fused_computation.7 | convolution fusion | flops 1077673984 | bytes 7866880 | tf_op jit(solution)/shard_map/dot_general | solution.py:60
  103.4 1.0 copy-done.7
  106.1 1.4 select_convert_fusion
  107.5 0.8 copy-done.5
  108.8 1.0 copy.66
  109.8 2.1 fusion.38
  112.0 2.3 fusion.26
  115.5 1.1 fusion.47
  116.6 1.0 fusion.48
  117.6 1.0 copy.67
  118.6 2.1 copy.68
  120.7 2.1 copy.69
  122.7 1.8 convolution_multiply_fusion
  124.6 6.2 %fusion.45 = (f32[256]{0:T(256)S(1)}, f32[256]{0:T(256)S(1)}, f32[256,1024]{1,0:T(8,128)S(1)}) fusion(f32[256]{0:T(256)S(1)} %add_rsqrt_fusion.1, f32[256]{0:T(256)S(1)} %broadcast_multiply_fusion.6, bf16[256,1024]{1,0:T(8,128)(2,1)S(1)} %copy-done.2, bf16[256]{0:T(256)(128)(2,1)S(1)} %gather_fusion.3, bf16[1024,2048]{1,0:T(8,128)(2,1)} %param.11, ...), kind=kOutput, calls=%fused_computation.101 | convolution fusion | flops 1081867776 | bytes 9966080 | tf_op jit(solution)/shard_map/dot_general | solution.py:45
  130.8 1.2 fusion.4
  132.0 1.4 fusion.14
  133.5 201.1 %all-reduce.3.cloned.1.call-done = f32[512,1024]{1,0:T(8,128)} async-done(((f32[512,1024]{1,0:T(8,128)}), f32[512,1024]{1,0:T(8,128)}) %all-reduce.3.cloned.1.call-update) | async-done | bytes 2097168
  335.4 45.1 %psum.8 = f32[8,1024]{1,0:T(8,128)} all-reduce(f32[8,1024]{1,0:T(8,128)S(1)} %constant_dynamic-slice_fusion), channel_id=1, replica_groups=mesh['dp'=12,'table'=64] {'dp'}, use_global_device_ids=true, to_apply=%region_14.15 | all-reduce | flops 8192 | bytes 65536 | tf_op jit(solution)/shard_map/psum | solution.py:132
  (69 shorter events, 6.9 us)
Async XLA Ops:
  7.2 43.4 %copy-start = (bf16[1024,1024]{1,0:T(8,128)(2,1)S(1)}, bf16[1024,1024]{1,0:T(8,128)(2,1)}, u32[]{:S(2)}) copy-start(bf16[1024,1024]{1,0:T(8,128)(2,1)} %param.9) | copy-start | bytes 6291460
  7.2 34.8 %copy-start.1 = (s32[1024]{0:T(1024)S(1)}, s32[1024]{0:T(1024)}, u32[]{:S(2)}) copy-start(s32[1024]{0:T(1024)} %param.10) | copy-start | bytes 12292
  45.1 14.1 %all-to-all-start.2 = ((bf16[64,1,8]{2,1,0:T(2,128)(2,1)}), bf16[64,1,8]{2,1,0:T(2,128)(2,1)S(1)}, u32[]{:S(2)}, u32[]{:S(2)}) async-start(bf16[64,1,8]{2,1,0:T(2,128)(2,1)} %convert_element_type.79), calls=%async_computation.2 | async-start | bytes 65536 | tf_op jit(solution)/shard_map/all_to_all | solution.py:123
  53.3 11.6 %copy-start.14 = (s32[1,4]{1,0:T(1,128)S(1)}, s32[1,4]{1,0:T(1,128)}, u32[]{:S(2)}) copy-start(s32[1,4]{1,0:T(1,128)} %param.8) | copy-start | bytes 52
  59.2 34.5 %all-to-all-start.1 = ((bf16[64,8,1024]{2,1,0:T(8,128)(2,1)}), bf16[64,8,1024]{2,1,0:T(8,128)(2,1)S(1)}, u32[]{:S(2)}, u32[]{:S(2)}) async-start(bf16[64,8,1024]{2,1,0:T(8,128)(2,1)} %bitcast.84), calls=%async_computation.1 | async-start | bytes 2097152 | tf_op jit(solution)/shard_map/all_to_all | solution.py:122
  64.7 269.9 %all-reduce.3.cloned.1.call-start = ((), (), s32[]{:S(2)}) async-start(), calls=%async_computation.3 | async-start | bytes 4194304
  103.4 1.0 copy-start.7
  105.4 0.7 copy-start.8
  106.1 2.2 copy-start.12
  107.5 0.8 copy-start.5
  107.5 2.3 copy-start.3
  109.8 2.2 copy-start.4
  109.8 4.4 %copy-start.6 = (bf16[4,256,256]{2,1,0:T(8,128)(2,1)S(1)}, bf16[4,256,256]{2,1,0:T(8,128)(2,1)}, u32[]{:S(2)}) copy-start(bf16[4,256,256]{2,1,0:T(8,128)(2,1)} %copy-done.5) | copy-start | bytes 1572868
  111.9 2.6 copy-start.13
  112.0 2.6 copy-start.15
  114.5 1.0 copy-start.9
  117.6 5.1 %copy-start.11 = (bf16[256,512]{1,0:T(8,128)(2,1)S(1)}, bf16[256,512]{1,0:T(8,128)(2,1)}, u32[]{:S(2)}) copy-start(bf16[256,512]{1,0:T(8,128)(2,1)} %get-tuple-element.10) | copy-start | bytes 786436
  122.7 1.8 copy-start.2
  124.6 6.2 %copy-start.10 = (bf16[512,1024]{1,0:T(8,128)(2,1)S(1)}, bf16[512,1024]{1,0:T(8,128)(2,1)}, u32[]{:S(2)}) copy-start(bf16[512,1024]{1,0:T(8,128)(2,1)} %param.12) | copy-start | bytes 3145732
Sparse Core Ops, SparseCore 0:
  124.7 209.8 all-reduce.2
where the time goes:
time: 388 us; the launch traced here: 387 us
  waiting for transfers between devices  231 us (60%)
  blocking collectives  66.5 us (17%)
  local copies, waits for them, and re-layouts  33.5 us (9%)
  matrix products  21.2 us (5%)
  between operations  15 us (4%)
  starting transfers between devices  11.3 us (3%)
  other arithmetic  8.59 us (2%)
    unnamed x2, waiting for transfers between devices  201 us
    psum x1, blocking collectives, on_device(): summed = lax.psum(scaled, 'dp')  45.1 us
    all_to_all x1, waiting for transfers between devices, on_device(): lax.all_to_all(looked_up, 'table', split_axis=0, concat_axis=0, tiled=True)  24.2 us
    all_to_all x1, blocking collectives, on_device(): lax.all_to_all(outgoing, 'table', split_axis=0, concat_axis=0, tiled=True)  21.5 us
    scatter x1, local copies, waits for them, and re-layouts, on_device(): jnp.zeros((shards, capacity), jnp.int32).at[owner_shard, slot_rank]  11.3 us
    dot_general x2, matrix products, contract_last(): lax.dot_general(left_side, right_side, (((1,), (1,)), ((), ())), preferre...  8.33 us
  transfers between devices with their start and end apart: 3, of which 3 were waited for; matrix products, arithmetic and copies ran while one was open for 4% of the time, Pallas kernels for 0%

commit v1 on v0

v1 whole, which is shorter than its diff:
```python
import functools
import math

import jax
import jax.numpy as jnp
from jax import lax
from jax.experimental import pallas as pl
from jax.experimental.pallas import tpu as pltpu
from jax.sharding import PartitionSpec as P

HEADS = 4
MOST = 128
CAP = 8
NX = 4
EPS = 1e-05
F32 = jnp.float32
BF16 = jnp.bfloat16
MESH = pl.DeviceIdType.MESH


def sigmoid(v):
    return 0.5 * jnp.tanh(0.5 * v) + 0.5


def mm(a, b, dims):
    return lax.dot_general(a, b, (dims, ((), ())), preferred_element_type=F32)


def iota(shape, dim):
    return lax.broadcasted_iota(jnp.int32, shape, dim)


def wait_bytes(ref, sem):
    pltpu.make_async_copy(ref, ref, sem).wait()


def kernel(
    nz, ns,
    ids_ref, len_ref, adm_ref, table_hbm, win_hbm, wout_hbm, og_hbm,
    lo_hbm, eg_hbm, wg_hbm,
    table_v, win_v, wout_v, og_v,
    req_s, req_r, flg_s, flg_r, rows_s, rows_r,
    perm, fet_v, nrm_f, nrm_b, proj, act, vism, sco, wts,
    att, hnorm, mix, gmix, gatt, gproj,
    wt_f, w1_s, w1_r, w2_s, w2_r, w3_s, w3_r, a2, a3, a4, r4, o4,
    lo_v, eg_v, wg_v,
    ld_sem, st_sem, ss, rs, rs1,
):
    ny = ns // (2 * NX)
    row = 2 * NX
    T, D = og_v.shape
    W = wout_v.shape[0]
    R = table_v.shape[0]
    H = D // 2
    hd = W // HEADS
    z = lax.axis_index("dp")
    me = lax.axis_index("table")
    core = me % 2
    x = (me // 2) % NX
    y = me // row

    bar = pltpu.get_barrier_semaphore()

    def sig_t(k, c):
        pl.semaphore_signal(bar, 1, device_id={"table": (me + k) % ns}, device_id_type=MESH)
        return c

    def sig_z(k, c):
        pl.semaphore_signal(bar, 1, device_id={"dp": (z + k) % nz}, device_id_type=MESH)
        return c

    lax.fori_loop(1, ns, sig_t, 0)
    lax.fori_loop(1, nz, sig_z, 0)

    loads = [
        pltpu.make_async_copy(table_hbm, table_v, ld_sem.at[0]),
        pltpu.make_async_copy(wout_hbm, wout_v, ld_sem.at[1]),
        pltpu.make_async_copy(og_hbm, og_v, ld_sem.at[2]),
        pltpu.make_async_copy(win_hbm, win_v, ld_sem.at[3]),
    ]
    for c in loads:
        c.start()

    ids_row = ids_ref[...]
    own_row = ids_row >> (R.bit_length() - 1)
    ri = iota((T, T), 0)
    ci = iota((T, T), 1)
    ids_col = jnp.sum(
        jnp.where(ri == ci, jnp.broadcast_to(ids_row.astype(F32), (T, T)), 0.0), axis=1, keepdims=True
    ).astype(jnp.int32)
    own_col = ids_col >> (R.bit_length() - 1)
    loc_col = ids_col & (R - 1)
    before = (own_col == own_row) & (ci < ri)
    rank_col = jnp.sum(jnp.where(before, 1.0, 0.0), axis=1, keepdims=True).astype(jnp.int32)
    owner_hot = jnp.where(iota((ns, T), 0) == own_row, 1.0, 0.0).astype(BF16)
    at_rank = iota((T, 128), 1) == rank_col
    hi = jnp.where(at_rank, (loc_col >> 5).astype(F32), 0.0).astype(BF16)
    lo = jnp.where(at_rank, (loc_col & 31).astype(F32), 0.0).astype(BF16)
    req = mm(owner_hot, hi, ((1,), (0,))) * 32.0 + mm(owner_hot, lo, ((1,), (0,)))
    for s in range(ns):
        req_s[s] = req[s : s + 1, :]
    req_r[me] = req_s[me]

    pl.semaphore_wait(bar, ns - 1 + nz - 1)

    def send_req(k, c):
        peer = (me + k) % ns
        pltpu.make_async_remote_copy(
            req_s.at[peer], req_r.at[me], ss.at[0], rs.at[0], device_id={"table": peer}, device_id_type=MESH
        ).start()
        return c

    lax.fori_loop(1, ns, send_req, 0)

    slot = own_col * (2 * CAP) + rank_col
    pi = iota((T, ns * 2 * CAP), 1)
    perm[pl.ds(0, T)] = jnp.where(pi == slot, 1.0, 0.0).astype(BF16)
    perm[pl.ds(T, T)] = jnp.where(pi == slot + CAP, 1.0, 0.0).astype(BF16)

    l0 = len_ref[0, 0]
    l1 = l0 + len_ref[0, 1]
    l2 = l1 + len_ref[0, 2]

    def segment(pos):
        one = jnp.where(pos >= l0, 1, 0)
        two = jnp.where(pos >= l1, 1, 0)
        return one + two + jnp.where(pos >= l2, 1, 0)

    vism[...] = jnp.where((segment(ri) == segment(ci)) & (ci <= ri), 1.0 / MOST, 0.0)

    loads[0].wait()
    adm = adm_ref[...].astype(F32)
    wait_bytes(req_r.at[pl.ds(0, ns - 1)], rs.at[0])
    half = max(ny // 2, 1)
    ones = jnp.ones((R, 128), BF16)
    for part in range(ny // half):
        hot = []
        for j in range(half):
            yy = (y + ny // 4 + part * half + j) % ny
            r = jnp.broadcast_to(req_r[pl.ds(yy * row, row)], (row, CAP, 128))
            r = jnp.where(iota((row, CAP, 128), 1) == iota((row, CAP, 128), 2), r, 0.0)
            r = jnp.sum(r, axis=2, keepdims=True).reshape(row * CAP, 1).astype(jnp.int32)
            hot.append(jnp.where(iota((row * CAP, R), 1) == r, adm, 0.0).astype(BF16))
        hot = jnp.concatenate(hot, axis=0)
        got = mm(hot, table_v[...], ((1,), (0,)))
        got = jnp.concatenate(
            [got[:, :H].reshape(half * row, CAP, H), got[:, H:].reshape(half * row, CAP, H)], axis=1
        ).astype(BF16)
        flg = mm(hot, ones, ((1,), (0,))).reshape(half * row, CAP, 128)
        flg = jnp.where(iota(flg.shape, 1) == iota(flg.shape, 2), flg, 0.0)
        flg = jnp.sum(flg, axis=1, keepdims=True)
        for j in range(half):
            yy = (y + ny // 4 + part * half + j) % ny
            rows_s[pl.ds(yy * row, row)] = got[j * row : (j + 1) * row]
            flg_s[pl.ds(yy * row, row)] = flg[j * row : (j + 1) * row]

        def send_rows(k, c):
            yy = (y + ny // 4 + part * half + k // row) % ny
            peer = yy * row + (me + k) % row

            @pl.when(peer != me)
            def _():
                pltpu.make_async_remote_copy(
                    rows_s.at[peer], rows_r.at[me], ss.at[1], rs.at[1],
                    device_id={"table": peer}, device_id_type=MESH,
                ).start()

            return c

        lax.fori_loop(0, half * row, send_rows, 0)

    def send_flg(k, c):
        peer = (me + k) % ns
        pltpu.make_async_remote_copy(
            flg_s.at[peer], flg_r.at[me], ss.at[2], rs.at[2], device_id={"table": peer}, device_id_type=MESH
        ).start()
        return c

    lax.fori_loop(1, ns, send_flg, 0)
    rows_r[me] = rows_s[me]
    flg_r[me] = flg_s[me]

    loads[1].wait()
    loads[2].wait()
    gmix[...] = mm(og_v[...], wout_v[...], ((1,), (1,)))
    loads[3].wait()

    wait_bytes(rows_r.at[pl.ds(0, ns - 1)], rs.at[1])
    got = mm(perm[...], rows_r[...].reshape(ns * 2 * CAP, H), ((1,), (0,)))
    fet = jnp.concatenate([got[:T], got[T:]], axis=1)
    fet_v[...] = fet
    cen = fet - jnp.sum(fet, axis=1, keepdims=True) * (1.0 / D)
    inv = lax.rsqrt(jnp.sum(cen * cen, axis=1, keepdims=True) * (1.0 / D) + EPS)
    nrm = cen * inv
    nrm_f[...] = nrm
    nrm_b[...] = nrm.astype(BF16)

    wide = min(256, 4 * W)
    for n in range(4 * W // wide):
        cols = slice(n * wide, (n + 1) * wide)
        p = mm(nrm_b[...], win_v[:, cols], ((1,), (0,)))
        proj[:, cols] = p
        act[:, cols] = (p * sigmoid(p)).astype(BF16)

    for h in range(HEADS):
        v = act[:, W + h * hd : W + (h + 1) * hd]
        q = act[:, 2 * W + h * hd : 2 * W + (h + 1) * hd]
        k = act[:, 3 * W + h * hd : 3 * W + (h + 1) * hd]
        s = mm(q, k, ((1,), (1,)))
        sco[h] = s
        w = (s * sigmoid(s) * vism[...]).astype(BF16)
        wts[h] = w
        att[:, h * hd : (h + 1) * hd] = mm(w, v, ((1,), (0,)))

    a = att[...]
    a = a - jnp.sum(a, axis=1, keepdims=True) * (1.0 / W)
    hscale = lax.rsqrt(jnp.sum(a * a, axis=1, keepdims=True) * (1.0 / W) + EPS)
    hn = a * hscale
    hnorm[...] = hn
    mix[...] = (hn * act[:, :W].astype(F32)).astype(BF16)

    factor = 1.0 / math.sqrt(T * nz * ns)
    for c in range(2):
        wt = mm(mix[...], og_v[:, c * H : (c + 1) * H], ((0,), (0,))) * factor
        wt = wt.reshape(ny, NX, 2, 8, H)
        for xx in range(NX):
            for cc in range(2):
                wt_f[cc, xx, :, c * 8 : (c + 1) * 8, :] = wt[:, xx, cc]

    partner = me + 1 - 2 * core
    pair = []
    for i in range(NX):
        xx = (x + NX // 2 + i) % NX
        w1_s[xx] = wt_f[1 - core, xx].astype(BF16)
        c = pltpu.make_async_remote_copy(
            w1_s.at[xx], w1_r.at[xx], ss.at[3], rs1.at[xx], device_id={"table": partner}, device_id_type=MESH
        )
        c.start()
        pair.append(c)

    lo_v[...] = (fet_v[...] + mm(mix[...], wout_v[...], ((1,), (0,)))).astype(BF16)
    put_lo = pltpu.make_async_copy(lo_v, lo_hbm, st_sem.at[0])
    put_lo.start()

    for i in range(NX):
        xx = (x + NX // 2 + i) % NX
        pltpu.make_async_copy(w1_r.at[xx], w1_r.at[xx], rs1.at[xx]).wait()
        total = wt_f[core, xx] + w1_r[xx].astype(F32)
        w2_s[xx] = total.astype(BF16)
        if i == NX - NX // 2:
            a2[...] = total
        else:
            pltpu.make_async_remote_copy(
                w2_s.at[xx], w2_r.at[x], ss.at[4], rs.at[3],
                device_id={"table": (y * NX + xx) * 2 + core}, device_id_type=MESH,
            ).start()

    g = gmix[...] * act[:, :W].astype(F32)
    hn = hnorm[...]
    g = g - jnp.sum(g, axis=1, keepdims=True) * (1.0 / W) - hn * (jnp.sum(g * hn, axis=1, keepdims=True) * (1.0 / W))
    gatt[...] = (hscale * g).astype(BF16)

    def through_silu(grad, at):
        p = proj[:, at : at + grad.shape[1]]
        s = sigmoid(p)
        gproj[:, at : at + grad.shape[1]] = (grad * (s * (1.0 + p * (1.0 - s)))).astype(BF16)

    through_silu(gmix[...] * hn, 0)

    wait_bytes(w2_r.at[pl.ds(0, NX - 1)], rs.at[3])
    w2_r[x] = jnp.zeros(w2_r.shape[1:], BF16)
    total = a2[...]
    for i in range(NX):
        total = total + w2_r[i].astype(F32)
    w3_s[...] = total.astype(BF16)
    a3[...] = total

    def send_y(k, c):
        yy = (y + k) % ny
        pltpu.make_async_remote_copy(
            w3_s.at[yy], w3_r.at[y], ss.at[5], rs.at[4],
            device_id={"table": (yy * NX + x) * 2 + core}, device_id_type=MESH,
        ).start()
        return c

    lax.fori_loop(1, ny, send_y, 0)

    for h in range(HEADS):
        v = act[:, W + h * hd : W + (h + 1) * hd]
        q = act[:, 2 * W + h * hd : 2 * W + (h + 1) * hd]
        k = act[:, 3 * W + h * hd : 3 * W + (h + 1) * hd]
        ga = gatt[:, h * hd : (h + 1) * hd]
        gw = mm(ga, v, ((1,), (1,)))
        gv = mm(wts[h], ga, ((0,), (0,)))
        sv = sco[h]
        s = sigmoid(sv)
        gs = (gw * (s * (1.0 + sv * (1.0 - s))) * vism[...]).astype(BF16)
        gq = mm(gs, k, ((1,), (0,)))
        gk = mm(gs, q, ((0,), (0,)))
        through_silu(gv, W + h * hd)
        through_silu(gq, 2 * W + h * hd)
        through_silu(gk, 3 * W + h * hd)

    wait_bytes(w3_r.at[pl.ds(0, ny - 1)], rs.at[4])
    w3_r[y] = jnp.zeros(w3_r.shape[1:], BF16)
    total = a3[y]
    for i in range(ny):
        total = total + w3_r[i].astype(F32)
    nt = D // 128
    for j in range(nt):
        c, at = divmod(j, nt // 2)
        a4[j] = total[c * 8 : (c + 1) * 8, at * 128 : (at + 1) * 128]

    @pl.when(z < nt)
    def _():
        r4[z] = a4[jnp.minimum(z, nt - 1)]

    for j in range(nt):

        @pl.when(z != j)
        def _():
            pltpu.make_async_remote_copy(
                a4.at[j], r4.at[z], ss.at[6], rs.at[5], device_id={"dp": j}, device_id_type=MESH
            ).start()

    gn = mm(gproj[...], win_v[...], ((1,), (1,)))
    nrm = nrm_f[...]
    m1 = jnp.sum(gn, axis=1, keepdims=True) * (1.0 / D)
    m2 = jnp.sum(gn * nrm, axis=1, keepdims=True) * (1.0 / D)
    wait_bytes(flg_r.at[pl.ds(0, ns - 1)], rs.at[2])
    flags = jnp.concatenate([flg_r[s] for s in range(ns)], axis=0).astype(BF16)
    own_hot = jnp.where(iota((T, ns), 1) == own_col, 1.0, 0.0).astype(BF16)
    flag = mm(own_hot, flags, ((1,), (0,)))
    flag = jnp.sum(jnp.where(at_rank, flag, 0.0), axis=1, keepdims=True)
    eg_v[...] = flag * (inv * (gn - m1 - nrm * m2) + og_v[...].astype(F32))
    put_eg = pltpu.make_async_copy(eg_v, eg_hbm, st_sem.at[1])
    put_eg.start()

    @pl.when(z < nt)
    def _():
        wait_bytes(r4.at[pl.ds(0, nz - 1)], rs.at[5])
        acc = r4[0]
        for i in range(1, nz):
            acc = acc + r4[i]
        zz = jnp.minimum(z, nt - 1)
        o4[zz] = acc

        def send_o(k, c):
            pltpu.make_async_remote_copy(
                o4.at[zz], o4.at[zz], ss.at[7], rs.at[6], device_id={"dp": (z + k) % nz}, device_id_type=MESH
            ).start()
            return c

        lax.fori_loop(1, nz, send_o, 0)
        wait_bytes(o4.at[pl.ds(0, nt - 1)], rs.at[6])
        wait_bytes(a4.at[pl.ds(0, nt - 1)], ss.at[6])
        wait_bytes(r4.at[pl.ds(0, nz - 1)], ss.at[7])

    @pl.when(z >= nt)
    def _():
        wait_bytes(o4, rs.at[6])
        wait_bytes(a4, ss.at[6])

    for j in range(nt):
        wg_v[:, j * 128 : (j + 1) * 128] = o4[j]
    put_wg = pltpu.make_async_copy(wg_v, wg_hbm, st_sem.at[2])
    put_wg.start()

    wait_bytes(req_s.at[pl.ds(0, ns - 1)], ss.at[0])
    wait_bytes(rows_s.at[pl.ds(0, ns - 1)], ss.at[1])
    wait_bytes(flg_s.at[pl.ds(0, ns - 1)], ss.at[2])
    wait_bytes(w1_s, ss.at[3])
    wait_bytes(w2_s.at[pl.ds(0, NX - 1)], ss.at[4])
    wait_bytes(w3_s.at[pl.ds(0, ny - 1)], ss.at[5])
    put_lo.wait()
    put_eg.wait()
    put_wg.wait()


def on_device(nz, item_ids, lengths, item_table, admitted, input_weight, output_weight, out_grad):
    ns = lax.axis_size("table")
    ny = ns // (2 * NX)
    T = item_ids.shape[0]
    R, D = item_table.shape
    W = output_weight.shape[0]
    H = D // 2
    nt = D // 128
    V = pltpu.VMEM
    vspec = pl.BlockSpec(memory_space=pltpu.VMEM)
    hspec = pl.BlockSpec(memory_space=pl.ANY)
    scratch = [
        V((R, D), BF16), V((D, 4 * W), BF16), V((W, D), BF16), V((T, D), BF16),
        V((ns, 1, 128), F32), V((ns, 1, 128), F32), V((ns, 1, 128), F32), V((ns, 1, 128), F32),
        V((ns, 2 * CAP, H), BF16), V((ns, 2 * CAP, H), BF16),
        V((2 * T, ns * 2 * CAP), BF16), V((T, D), F32), V((T, D), F32), V((T, D), BF16),
        V((T, 4 * W), F32), V((T, 4 * W), BF16), V((T, T), F32), V((HEADS, T, T), F32), V((HEADS, T, T), BF16),
        V((T, W), F32), V((T, W), F32), V((T, W), BF16), V((T, W), F32), V((T, W), BF16), V((T, 4 * W), BF16),
        V((2, NX, ny, 16, H), F32), V((NX, ny, 16, H), BF16), V((NX, ny, 16, H), BF16),
        V((NX, ny, 16, H), BF16), V((NX, ny, 16, H), BF16), V((ny, 16, H), BF16), V((ny, 16, H), BF16),
        V((ny, 16, H), F32), V((ny, 16, H), F32), V((nt, 8, 128), F32), V((nz, 8, 128), F32), V((nt, 8, 128), F32),
        V((T, D), BF16), V((T, D), F32), V((8, D), F32),
        pltpu.SemaphoreType.DMA((4,)), pltpu.SemaphoreType.DMA((3,)),
        pltpu.SemaphoreType.DMA((8,)), pltpu.SemaphoreType.DMA((7,)), pltpu.SemaphoreType.DMA((NX,)),
    ]
    return pl.pallas_call(
        functools.partial(kernel, nz, ns),
        out_shape=(
            jax.ShapeDtypeStruct((T, D), BF16),
            jax.ShapeDtypeStruct((T, D), F32),
            jax.ShapeDtypeStruct((8, D), F32),
        ),
        in_specs=[vspec, pl.BlockSpec(memory_space=pltpu.SMEM), vspec, hspec, hspec, hspec, hspec],
        out_specs=(hspec, hspec, hspec),
        scratch_shapes=scratch,
        compiler_params=pltpu.CompilerParams(
            collective_id=0, has_side_effects=True, vmem_limit_bytes=56 * 1024 * 1024
        ),
        name="layer",
    )(
        item_ids.reshape(1, T), lengths, admitted.reshape(1, R), item_table, input_weight, output_weight, out_grad
    )


def solution(mesh):
    return jax.shard_map(
        functools.partial(on_device, mesh.shape["dp"]),
        mesh=mesh,
        in_specs=(
            P(("dp", "table")),
            P(("dp", "table"), None),
            P("table", None),
            P("table"),
            P(),
            P(),
            P(("dp", "table"), None),
        ),
        out_specs=(P(("dp", "table"), None), P(("dp", "table"), None), P("table", None)),
        check_vma=False,
    )
```

time: 388 us -> 90.7 us (0.23)
  the two profiles are of different devices: /device:TPU:2 before, /device:TPU:16 now
where the time goes in v1:
time: 90.7 us; the launch traced here: 90.4 us
  Pallas kernels  84.2 us (93%)
  local copies, waits for them, and re-layouts  5.55 us (6%)
    pallas_call x1, Pallas kernels, on_device(): pl.pallas_call(functools.partial(kernel, nz, ns), out_shape=(jax.ShapeDty...  84.2 us
    unnamed x3, local copies, waits for them, and re-layouts  5.55 us

profile of v1, /device:TPU:16, one launch (start us, length us, event | category | flops | bytes accessed | tf_op | source)
XLA Modules:
  0.0 90.4 jit_solution(13033667212058507697)
XLA Ops:
  0.6 84.2 %layer.1 = (bf16[256,1024]{1,0:T(8,128)(2,1)}, f32[256,1024]{1,0:T(8,128)}, f32[8,1024]{1,0:T(8,128)}) custom-call(s32[1,256]{1,0:T(1,128)} %bitcast.3, s32[1,4]{1,0:T(1,128)} %len_ref.1, s32[1,1024]{1,0:T(1,128)} %bitcast.2, bf16[1024,1024]{1,0:T(8,128)(2,1)} %table_hbm.1, bf16[1024,2048]{1,0:T(8,128)(2,1)} %win_hbm.1, bf16[512,1024]{1,0:T(8,128)(2,1)} %wout_hbm.1, ...), custom_call_target="tpu_custom_call" | custom-call | tf_op jit(solution)/shard_map/layer/pallas_call | solution.py:405
  84.8 1.9 %copy.13 = bf16[256,1024]{1,0:T(8,128)(2,1)} copy(bf16[256,1024]{1,0:T(8,128)(2,1)} %get-tuple-element.6) | data formatting | bytes 1048576
  86.7 2.3 %copy.14 = f32[256,1024]{1,0:T(8,128)} copy(f32[256,1024]{1,0:T(8,128)} %get-tuple-element.7) | data formatting | bytes 2097152
  89.0 1.4 %copy.15 = f32[8,1024]{1,0:T(8,128)} copy(f32[8,1024]{1,0:T(8,128)} %get-tuple-element.8) | data formatting | bytes 65536

commit v2 on v1

v2 whole, which is shorter than its diff:
```python
import functools
import math

import jax
import jax.numpy as jnp
from jax import lax
from jax.experimental import pallas as pl
from jax.experimental.pallas import tpu as pltpu
from jax.sharding import PartitionSpec as P

HEADS = 4
MOST = 128
CAP = 8
NX = 4
EPS = 1e-05
F32 = jnp.float32
BF16 = jnp.bfloat16
MESH = pl.DeviceIdType.MESH


def sigmoid(v):
    return 0.5 * jnp.tanh(0.5 * v) + 0.5


def mm(a, b, dims):
    return lax.dot_general(a, b, (dims, ((), ())), preferred_element_type=F32)


def iota(shape, dim):
    return lax.broadcasted_iota(jnp.int32, shape, dim)


def wait_bytes(ref, sem):
    pltpu.make_async_copy(ref, ref, sem).wait()


def groups(ny):
    return [(1, 7), (4, 3), (5, 2), (6, 0)] if ny == 8 else [((k + 1) % ny,) for k in range(ny)]


def z_split(nz):
    near = 4 if nz % 4 == 0 else 1
    return near, nz // near


def kernel(
    nz, ns,
    ids_ref, len_ref, adm_ref, table_hbm, win_hbm, wout_hbm, og_hbm,
    lo_v, eg_v, wg_v,
    table_v, win_v, wout_v, og_v,
    req_s, req_r, flg_s, flg_r, rows_s, rows_r,
    perm, fet_v, nrm_f, nrm_b, proj, act, vism, sco, wts,
    att, hnorm, mix, gmix, gatt, gproj,
    wt_f, w1_s, w1_r, xa_s, xa_r, yb_s, yb_r, ya_s, ya_r, xb_s, xb_r,
    own_xa, own_ya, zr, zg,
    ld_sem, ss, rs, rs_req, rs1,
):
    ny = ns // (2 * NX)
    row = 2 * NX
    T, D = og_v.shape
    W = wout_v.shape[0]
    R = table_v.shape[0]
    H = D // 2
    HA = xa_s.shape[-1]
    hd = W // HEADS
    z = lax.axis_index("dp")
    me = lax.axis_index("table")
    core = me % 2
    x = (me // 2) % NX
    y = me // row
    near, far = z_split(nz)
    zl = z % near
    zg_me = z // near

    def copy(src, dst, i, to, sem=None):
        c = pltpu.make_async_remote_copy(
            src, dst, ss.at[i], rs.at[i] if sem is None else sem, device_id=to, device_id_type=MESH
        )
        c.start()

    bar = pltpu.get_barrier_semaphore()

    def sig_t(k, c):
        pl.semaphore_signal(bar, 1, device_id={"table": (me + k) % ns}, device_id_type=MESH)
        return c

    lax.fori_loop(3 * ns // 8, ns, sig_t, 0)
    lax.fori_loop(1, 3 * ns // 8, sig_t, 0)
    near_z = [zg_me * near + (zl + i) % near for i in range(1, near)]
    far_z = [((zg_me + i) % far) * near + zl for i in range(1, far)]
    for to in near_z + far_z:
        pl.semaphore_signal(bar, 1, device_id={"dp": to}, device_id_type=MESH)

    loads = [
        pltpu.make_async_copy(table_hbm, table_v, ld_sem.at[0]),
        pltpu.make_async_copy(wout_hbm, wout_v, ld_sem.at[1]),
        pltpu.make_async_copy(og_hbm, og_v, ld_sem.at[2]),
        pltpu.make_async_copy(win_hbm, win_v, ld_sem.at[3]),
    ]
    loads[0].start()

    ids_row = ids_ref[...]
    own_row = ids_row >> (R.bit_length() - 1)
    ri = iota((T, T), 0)
    ci = iota((T, T), 1)
    ids_col = jnp.sum(
        jnp.where(ri == ci, jnp.broadcast_to(ids_row.astype(F32), (T, T)), 0.0), axis=1, keepdims=True
    ).astype(jnp.int32)
    own_col = ids_col >> (R.bit_length() - 1)
    loc_col = ids_col & (R - 1)
    before = (own_col == own_row) & (ci < ri)
    rank_col = jnp.sum(jnp.where(before, 1.0, 0.0), axis=1, keepdims=True).astype(jnp.int32)
    owner_hot = jnp.where(iota((ns, T), 0) == own_row, 1.0, 0.0).astype(BF16)
    at_rank = iota((T, 128), 1) == rank_col
    hi = jnp.where(at_rank, (loc_col >> 5).astype(F32), 0.0).astype(BF16)
    lo = jnp.where(at_rank, (loc_col & 31).astype(F32), 0.0).astype(BF16)
    req = mm(owner_hot, hi, ((1,), (0,))) * 32.0 + mm(owner_hot, lo, ((1,), (0,)))
    for s in range(ns):
        req_s[s] = req[s : s + 1, :]
    req_r[me] = req_s[me]

    pl.semaphore_wait(bar, ns - 1 + len(near_z) + len(far_z))

    for gi, dys in enumerate(groups(ny)):
        for dy in dys:

            def send_req(k, c):
                peer = ((y + ny - dy) % ny) * row + (me + k) % row
                copy(req_s.at[peer], req_r.at[me], 0, {"table": peer}, rs_req.at[gi])
                return c

            lax.fori_loop(0 if dy else 1, row, send_req, 0)

    for c in loads[1:]:
        c.start()

    slot = own_col * (2 * CAP) + rank_col
    pi = iota((T, ns * 2 * CAP), 1)
    perm[pl.ds(0, T)] = jnp.where(pi == slot, 1.0, 0.0).astype(BF16)
    perm[pl.ds(T, T)] = jnp.where(pi == slot + CAP, 1.0, 0.0).astype(BF16)

    l0 = len_ref[0, 0]
    l1 = l0 + len_ref[0, 1]
    l2 = l1 + len_ref[0, 2]

    def segment(pos):
        one = jnp.where(pos >= l0, 1, 0)
        two = jnp.where(pos >= l1, 1, 0)
        return one + two + jnp.where(pos >= l2, 1, 0)

    vism[...] = jnp.where((segment(ri) == segment(ci)) & (ci <= ri), 1.0 / MOST, 0.0)

    loads[0].wait()
    adm = adm_ref[...].astype(F32)
    ones = jnp.ones((R, 128), BF16)
    for gi, dys in enumerate(groups(ny)):
        n = len(dys)
        wait_bytes(req_r.at[pl.ds(0, n * row - (0 in dys))], rs_req.at[gi])
        hot = []
        for dy in dys:
            yy = (y + dy) % ny
            r = jnp.broadcast_to(req_r[pl.ds(yy * row, row)], (row, CAP, 128))
            r = jnp.where(iota((row, CAP, 128), 1) == iota((row, CAP, 128), 2), r, 0.0)
            r = jnp.sum(r, axis=2, keepdims=True).reshape(row * CAP, 1).astype(jnp.int32)
            hot.append(jnp.where(iota((row * CAP, R), 1) == r, adm, 0.0).astype(BF16))
        hot = jnp.concatenate(hot, axis=0)
        got = mm(hot, table_v[...], ((1,), (0,)))
        got = jnp.concatenate(
            [got[:, :H].reshape(n * row, CAP, H), got[:, H:].reshape(n * row, CAP, H)], axis=1
        ).astype(BF16)
        for j, dy in enumerate(dys):
            yy = (y + dy) % ny
            rows_s[pl.ds(yy * row, row)] = got[j * row : (j + 1) * row]

        for dy in dys:

            def send_rows(k, c):
                peer = ((y + dy) % ny) * row + (me + k) % row
                copy(rows_s.at[peer], rows_r.at[me], 1, {"table": peer})
                return c

            lax.fori_loop(0 if dy else 1, row, send_rows, 0)
        flg = mm(hot, ones, ((1,), (0,))).reshape(n * row, CAP, 128)
        flg = jnp.where(iota(flg.shape, 1) == iota(flg.shape, 2), flg, 0.0)
        flg = jnp.sum(flg, axis=1, keepdims=True)
        for j, dy in enumerate(dys):
            yy = (y + dy) % ny
            flg_s[pl.ds(yy * row, row)] = flg[j * row : (j + 1) * row]

    def send_flg(k, c):
        peer = (me + k) % ns
        copy(flg_s.at[peer], flg_r.at[me], 2, {"table": peer})
        return c

    lax.fori_loop(1, ns, send_flg, 0)
    rows_r[me] = rows_s[me]
    flg_r[me] = flg_s[me]

    loads[1].wait()
    loads[2].wait()
    gmix[...] = mm(og_v[...], wout_v[...], ((1,), (1,)))
    loads[3].wait()

    wait_bytes(rows_r.at[pl.ds(0, ns - 1)], rs.at[1])
    got = mm(perm[...], rows_r[...].reshape(ns * 2 * CAP, H), ((1,), (0,)))
    fet = jnp.concatenate([got[:T], got[T:]], axis=1)
    fet_v[...] = fet
    cen = fet - jnp.sum(fet, axis=1, keepdims=True) * (1.0 / D)
    inv = lax.rsqrt(jnp.sum(cen * cen, axis=1, keepdims=True) * (1.0 / D) + EPS)
    nrm = cen * inv
    nrm_f[...] = nrm
    nrm_b[...] = nrm.astype(BF16)

    wide = min(256, 4 * W)
    for n in range(4 * W // wide):
        cols = slice(n * wide, (n + 1) * wide)
        p = mm(nrm_b[...], win_v[:, cols], ((1,), (0,)))
        proj[:, cols] = p
        act[:, cols] = (p * sigmoid(p)).astype(BF16)

    for h in range(HEADS):
        v = act[:, W + h * hd : W + (h + 1) * hd]
        q = act[:, 2 * W + h * hd : 2 * W + (h + 1) * hd]
        k = act[:, 3 * W + h * hd : 3 * W + (h + 1) * hd]
        s = mm(q, k, ((1,), (1,)))
        sco[h] = s
        w = (s * sigmoid(s) * vism[...]).astype(BF16)
        wts[h] = w
        att[:, h * hd : (h + 1) * hd] = mm(w, v, ((1,), (0,)))

    a = att[...]
    a = a - jnp.sum(a, axis=1, keepdims=True) * (1.0 / W)
    hscale = lax.rsqrt(jnp.sum(a * a, axis=1, keepdims=True) * (1.0 / W) + EPS)
    hn = a * hscale
    hnorm[...] = hn
    mix[...] = (hn * act[:, :W].astype(F32)).astype(BF16)

    factor = 1.0 / math.sqrt(T * nz * ns)
    for c in range(2):
        wt = mm(mix[...], og_v[:, c * H : (c + 1) * H], ((0,), (0,))) * factor
        wt = wt.reshape(ny, NX, 2, 8, H)
        for xx in range(NX):
            for cc in range(2):
                wt_f[cc, xx, :, c * 8 : (c + 1) * 8, :] = wt[:, xx, cc]

    partner = me + 1 - 2 * core
    for i in range(NX):
        xx = (x + NX // 2 + i) % NX
        w1_s[xx] = wt_f[1 - core, xx].astype(BF16)
        copy(w1_s.at[xx], w1_r.at[xx], 3, {"table": partner}, rs1.at[xx])

    lo_v[...] = (fet_v[...] + mm(mix[...], wout_v[...], ((1,), (0,)))).astype(BF16)

    for i in range(NX):
        xx = (x + NX // 2 + i) % NX
        wait_bytes(w1_r.at[xx], rs1.at[xx])
        total = wt_f[core, xx] + w1_r[xx].astype(F32)
        yb_s[:, xx] = total[..., HA:].astype(BF16)
        if i == NX - NX // 2:
            own_xa[...] = total[..., :HA]
        else:
            xa_s[xx] = total[..., :HA].astype(BF16)
            copy(xa_s.at[xx], xa_r.at[x], 4, {"table": (y * NX + xx) * 2 + core})
    xa_r[x] = jnp.zeros(xa_r.shape[1:], BF16)

    def send_yb(k, c):
        yy = (y + k) % ny
        copy(yb_s.at[yy], yb_r.at[y], 5, {"table": (yy * NX + x) * 2 + core})
        return c

    lax.fori_loop(1, ny, send_yb, 0)
    yb_r[y] = yb_s[y]

    g = gmix[...] * act[:, :W].astype(F32)
    hn = hnorm[...]
    g = g - jnp.sum(g, axis=1, keepdims=True) * (1.0 / W) - hn * (jnp.sum(g * hn, axis=1, keepdims=True) * (1.0 / W))
    gatt[...] = (hscale * g).astype(BF16)

    def through_silu(grad, at):
        p = proj[:, at : at + grad.shape[1]]
        s = sigmoid(p)
        gproj[:, at : at + grad.shape[1]] = (grad * (s * (1.0 + p * (1.0 - s)))).astype(BF16)

    through_silu(gmix[...] * hn, 0)
    for h in range(HEADS):
        v = act[:, W + h * hd : W + (h + 1) * hd]
        q = act[:, 2 * W + h * hd : 2 * W + (h + 1) * hd]
        k = act[:, 3 * W + h * hd : 3 * W + (h + 1) * hd]
        ga = gatt[:, h * hd : (h + 1) * hd]
        gw = mm(ga, v, ((1,), (1,)))
        gv = mm(wts[h], ga, ((0,), (0,)))
        sv = sco[h]
        s = sigmoid(sv)
        gs = (gw * (s * (1.0 + sv * (1.0 - s))) * vism[...]).astype(BF16)
        gq = mm(gs, k, ((1,), (0,)))
        gk = mm(gs, q, ((0,), (0,)))
        through_silu(gv, W + h * hd)
        through_silu(gq, 2 * W + h * hd)
        through_silu(gk, 3 * W + h * hd)

    wait_bytes(xa_r.at[pl.ds(0, NX - 1)], rs.at[4])
    total = own_xa[...]
    for i in range(NX):
        total = total + xa_r[i].astype(F32)
    ya_s[...] = total.astype(BF16)
    own_ya[...] = total

    def send_ya(k, c):
        yy = (y + k) % ny
        copy(ya_s.at[yy], ya_r.at[y], 6, {"table": (yy * NX + x) * 2 + core})
        return c

    lax.fori_loop(1, ny, send_ya, 0)
    ya_r[y] = jnp.zeros(ya_r.shape[1:], BF16)
    wait_bytes(yb_r.at[pl.ds(0, ny - 1)], rs.at[5])
    total = yb_r[0].astype(F32)
    for i in range(1, ny):
        total = total + yb_r[i].astype(F32)
    xb_s[...] = total.astype(BF16)
    for i in range(1, NX):
        xx = (x + i) % NX
        copy(xb_s.at[xx], xb_r.at[x], 7, {"table": (y * NX + xx) * 2 + core})
    xb_r[x] = xb_s[x]

    gn = mm(gproj[...], win_v[...], ((1,), (1,)))
    nrm = nrm_f[...]
    m1 = jnp.sum(gn, axis=1, keepdims=True) * (1.0 / D)
    m2 = jnp.sum(gn * nrm, axis=1, keepdims=True) * (1.0 / D)
    wait_bytes(flg_r.at[pl.ds(0, ns - 1)], rs.at[2])
    flags = jnp.concatenate([flg_r[s] for s in range(ns)], axis=0).astype(BF16)
    own_hot = jnp.where(iota((T, ns), 1) == own_col, 1.0, 0.0).astype(BF16)
    flag = mm(own_hot, flags, ((1,), (0,)))
    flag = jnp.sum(jnp.where(at_rank, flag, 0.0), axis=1, keepdims=True)
    eg_v[...] = flag * (inv * (gn - m1 - nrm * m2) + og_v[...].astype(F32))

    wait_bytes(ya_r.at[pl.ds(0, ny - 1)], rs.at[6])
    total = own_ya[y]
    for i in range(ny):
        total = total + ya_r[i].astype(F32)
    zr[zl, :, pl.ds(0, HA)] = total.astype(BF16)
    wait_bytes(xb_r.at[pl.ds(0, NX - 1)], rs.at[7])
    total = xb_r[0].astype(F32)
    for i in range(1, NX):
        total = total + xb_r[i].astype(F32)
    zr[zl, :, pl.ds(HA, H - HA)] = total.astype(BF16)
    for to in near_z:
        copy(zr.at[zl], zr.at[zl], 8, {"dp": to})
    if near > 1:
        wait_bytes(zr.at[pl.ds(0, near - 1)], rs.at[8])
    total = zr[0].astype(F32)
    for i in range(1, near):
        total = total + zr[i].astype(F32)
    zg[zg_me] = total.astype(BF16)
    for to in far_z:
        copy(zg.at[zg_me], zg.at[zg_me], 9, {"dp": to})
    if far > 1:
        wait_bytes(zg.at[pl.ds(0, far - 1)], rs.at[9])
    total = zg[0].astype(F32)
    for i in range(1, far):
        total = total + zg[i].astype(F32)
    wg_v[:, :H] = total[:8]
    wg_v[:, H:] = total[8:]

    wait_bytes(req_s.at[pl.ds(0, ns - 1)], ss.at[0])
    wait_bytes(rows_s.at[pl.ds(0, ns - 1)], ss.at[1])
    wait_bytes(flg_s.at[pl.ds(0, ns - 1)], ss.at[2])
    wait_bytes(w1_s, ss.at[3])
    wait_bytes(xa_s.at[pl.ds(0, NX - 1)], ss.at[4])
    wait_bytes(yb_s.at[pl.ds(0, ny - 1)], ss.at[5])
    wait_bytes(ya_s.at[pl.ds(0, ny - 1)], ss.at[6])
    wait_bytes(xb_s.at[pl.ds(0, NX - 1)], ss.at[7])
    if near > 1:
        wait_bytes(zr.at[pl.ds(0, near - 1)], ss.at[8])
    if far > 1:
        wait_bytes(zg.at[pl.ds(0, far - 1)], ss.at[9])


def write_out(lo, eg, wg, lo_out, eg_out, wg_out, sems):
    copies = [
        pltpu.make_async_copy(a, b, sems.at[i])
        for i, (a, b) in enumerate(((eg, eg_out), (lo, lo_out), (wg, wg_out)))
    ]
    for c in copies:
        c.start()
    for c in copies:
        c.wait()


def on_device(nz, item_ids, lengths, item_table, admitted, input_weight, output_weight, out_grad):
    ns = lax.axis_size("table")
    ny = ns // (2 * NX)
    T = item_ids.shape[0]
    R, D = item_table.shape
    W = output_weight.shape[0]
    H = D // 2
    HA = H - H // 4 if H >= 512 else H // 2
    near, far = z_split(nz)
    V = pltpu.VMEM
    vspec = pl.BlockSpec(memory_space=pltpu.VMEM)
    hspec = pl.BlockSpec(memory_space=pltpu.HBM)
    scratch = [
        V((R, D), BF16), V((D, 4 * W), BF16), V((W, D), BF16), V((T, D), BF16),
        V((ns, 1, 128), F32), V((ns, 1, 128), F32), V((ns, 1, 128), F32), V((ns, 1, 128), F32),
        V((ns, 2 * CAP, H), BF16), V((ns, 2 * CAP, H), BF16),
        V((2 * T, ns * 2 * CAP), BF16), V((T, D), F32), V((T, D), F32), V((T, D), BF16),
        V((T, 4 * W), F32), V((T, 4 * W), BF16), V((T, T), F32), V((HEADS, T, T), F32), V((HEADS, T, T), BF16),
        V((T, W), F32), V((T, W), F32), V((T, W), BF16), V((T, W), F32), V((T, W), BF16), V((T, 4 * W), BF16),
        V((2, NX, ny, 16, H), F32), V((NX, ny, 16, H), BF16), V((NX, ny, 16, H), BF16),
        V((NX, ny, 16, HA), BF16), V((NX, ny, 16, HA), BF16),
        V((ny, NX, 16, H - HA), BF16), V((ny, NX, 16, H - HA), BF16),
        V((ny, 16, HA), BF16), V((ny, 16, HA), BF16),
        V((NX, 16, H - HA), BF16), V((NX, 16, H - HA), BF16),
        V((ny, 16, HA), F32), V((ny, 16, HA), F32), V((near, 16, H), BF16), V((far, 16, H), BF16),
        pltpu.SemaphoreType.DMA((4,)),
        pltpu.SemaphoreType.DMA((10,)), pltpu.SemaphoreType.DMA((10,)),
        pltpu.SemaphoreType.DMA((len(groups(ny)),)), pltpu.SemaphoreType.DMA((NX,)),
    ]
    results = pl.pallas_call(
        functools.partial(kernel, nz, ns),
        out_shape=(V((T, D), BF16), V((T, D), F32), V((8, D), F32)),
        in_specs=[vspec, pl.BlockSpec(memory_space=pltpu.SMEM), vspec, hspec, hspec, hspec, hspec],
        out_specs=(vspec, vspec, vspec),
        scratch_shapes=scratch,
        compiler_params=pltpu.CompilerParams(
            collective_id=0, has_side_effects=True, vmem_limit_bytes=60 * 1024 * 1024
        ),
        name="layer",
    )(
        item_ids.reshape(1, T), lengths, admitted.reshape(1, R), item_table, input_weight, output_weight, out_grad
    )
    return pl.pallas_call(
        write_out,
        out_shape=(
            jax.ShapeDtypeStruct((T, D), BF16),
            jax.ShapeDtypeStruct((T, D), F32),
            jax.ShapeDtypeStruct((8, D), F32),
        ),
        in_specs=[vspec] * 3,
        out_specs=(hspec,) * 3,
        scratch_shapes=[pltpu.SemaphoreType.DMA((3,))],
        compiler_params=pltpu.CompilerParams(vmem_limit_bytes=16 * 1024 * 1024),
        name="write_out",
    )(*results)


def solution(mesh):
    return jax.shard_map(
        functools.partial(on_device, mesh.shape["dp"]),
        mesh=mesh,
        in_specs=(
            P(("dp", "table")),
            P(("dp", "table"), None),
            P("table", None),
            P("table"),
            P(),
            P(),
            P(("dp", "table"), None),
        ),
        out_specs=(P(("dp", "table"), None), P(("dp", "table"), None), P("table", None)),
        check_vma=False,
    )
```

time: 90.7 us -> 78.6 us (0.87)
  the two profiles are of different devices: /device:TPU:16 before, /device:TPU:8 now
where the time goes in v2:
time: 78.6 us; the launch traced here: 78.4 us
  Pallas kernels  77.8 us (99%)
    pallas_call x1, Pallas kernels, on_device(): pl.pallas_call(functools.partial(kernel, nz, ns), out_shape=(V((T, D), BF...  76.6 us

profile of v2, /device:TPU:8, one launch (start us, length us, event | category | flops | bytes accessed | tf_op | source)
XLA Modules:
  0.0 78.4 jit_solution(3871378733687518412)
XLA Ops:
  0.6 76.6 %layer.1 = (bf16[256,1024]{1,0:T(8,128)(2,1)S(1)}, f32[256,1024]{1,0:T(8,128)S(1)}, f32[8,1024]{1,0:T(8,128)S(1)}) custom-call(s32[1,256]{1,0:T(1,128)} %bitcast.3, s32[1,4]{1,0:T(1,128)} %len_ref.1, s32[1,1024]{1,0:T(1,128)} %bitcast.2, bf16[1024,1024]{1,0:T(8,128)(2,1)} %table_hbm.1, bf16[1024,2048]{1,0:T(8,128)(2,1)} %win_hbm.1, ...), custom_call_target="tpu_custom_call" | custom-call | tf_op jit(solution)/shard_map/layer/pallas_call | solution.py:418
  77.3 1.2 %write_out.1 = (bf16[256,1024]{1,0:T(8,128)(2,1)}, f32[256,1024]{1,0:T(8,128)}, f32[8,1024]{1,0:T(8,128)}) custom-call(bf16[256,1024]{1,0:T(8,128)(2,1)S(1)} %get-tuple-element.6.lo, f32[256,1024]{1,0:T(8,128)S(1)} %get-tuple-element.7.eg, f32[8,1024]{1,0:T(8,128)S(1)} %get-tuple-element.8.wg), custom_call_target="tpu_custom_call" | custom-call | tf_op jit(solution)/shard_map/write_out/pallas_call | solution.py:431

commit v3 on v2

v3 whole, which is shorter than its diff:
```python
import functools
import math

import jax
import jax.numpy as jnp
from jax import lax
from jax.experimental import pallas as pl
from jax.experimental.pallas import tpu as pltpu
from jax.sharding import PartitionSpec as P

HEADS = 4
MOST = 128
CAP = 8
NX = 4
EPS = 1e-05
F32 = jnp.float32
BF16 = jnp.bfloat16
MESH = pl.DeviceIdType.MESH


def sigmoid(v):
    return 0.5 * jnp.tanh(0.5 * v) + 0.5


def mm(a, b, dims):
    return lax.dot_general(a, b, (dims, ((), ())), preferred_element_type=F32)


rem = lax.rem


def iota(shape, dim):
    return lax.broadcasted_iota(jnp.int32, shape, dim)


def wait_bytes(ref, sem):
    pltpu.make_async_copy(ref, ref, sem).wait()


def groups(ny):
    return [(1, 7), (4, 3), (5, 2), (6, 0)] if ny == 8 else [((k + 1) % ny,) for k in range(ny)]


def z_split(nz):
    near = 4 if nz % 4 == 0 else 1
    return near, nz // near


def kernel(
    nz, ns,
    ids_hbm, len_hbm, adm_hbm, table_hbm, win_hbm, wout_hbm, og_hbm,
    lo_v, eg_v, wg_v,
    ids_ref, len_ref, adm_ref, table_v, win_v, wout_v, og_v,
    req_s, req_r, flg_s, flg_r, rows_s, rows_r,
    perm, fet_v, nrm_f, nrm_b, proj, act, vism, sco, wts,
    att, hnorm, mix, gmix, gatt, gproj,
    wt_f, w1_s, w1_r, xa1_s, xa1_r, xa2_s, xa2_r, yb_s, yb_r, ya1_s, ya1_r, ya2_s, ya2_r, xb_s, xb_r,
    zr1, zr2, zg1, zg2,
    acc, ld_sem, ss, rs, rs_req, rs_rows, rs1,
):
    ny = ns // (2 * NX)
    row = 2 * NX
    T, D = og_v.shape
    W = wout_v.shape[0]
    R = table_v.shape[0]
    H = D // 2
    hd = W // HEADS
    z = lax.axis_index("dp")
    me = lax.axis_index("table")
    core = rem(me, 2)
    x = rem(me // 2, NX)
    y = me // row
    near, far = z_split(nz)
    zl = z % near
    zg_me = z // near

    def copy(src, dst, i, to, sem=None):
        c = pltpu.make_async_remote_copy(
            src, dst, ss.at[i], rs.at[i] if sem is None else sem, device_id=to, device_id_type=MESH
        )
        c.start()

    bar = pltpu.get_barrier_semaphore()

    def sig_t(k, c):
        pl.semaphore_signal(bar, 1, device_id={"table": rem(me + k, ns)}, device_id_type=MESH)
        return c

    lax.fori_loop(3 * ns // 8, ns, sig_t, 0)
    lax.fori_loop(1, 3 * ns // 8, sig_t, 0)
    near_z = [zg_me * near + (zl + i) % near for i in range(1, near)]
    far_z = [((zg_me + i) % far) * near + zl for i in range(1, far)]
    for to in near_z + far_z:
        pl.semaphore_signal(bar, 1, device_id={"dp": to}, device_id_type=MESH)

    loads = [
        pltpu.make_async_copy(table_hbm, table_v, ld_sem.at[0]),
        pltpu.make_async_copy(wout_hbm, wout_v, ld_sem.at[1]),
        pltpu.make_async_copy(og_hbm, og_v, ld_sem.at[2]),
        pltpu.make_async_copy(win_hbm, win_v, ld_sem.at[3]),
        pltpu.make_async_copy(ids_hbm, ids_ref, ld_sem.at[4]),
        pltpu.make_async_copy(len_hbm, len_ref, ld_sem.at[5]),
        pltpu.make_async_copy(adm_hbm, adm_ref, ld_sem.at[6]),
    ]
    for i in (4, 0, 6, 5):
        loads[i].start()

    loads[4].wait()
    ids_row = ids_ref[...]
    own_row = ids_row >> (R.bit_length() - 1)
    ri = iota((T, T), 0)
    ci = iota((T, T), 1)
    ids_col = jnp.sum(
        jnp.where(ri == ci, jnp.broadcast_to(ids_row.astype(F32), (T, T)), 0.0), axis=1, keepdims=True
    ).astype(jnp.int32)
    own_col = ids_col >> (R.bit_length() - 1)
    loc_col = ids_col & (R - 1)
    before = (own_col == own_row) & (ci < ri)
    rank_col = jnp.sum(jnp.where(before, 1.0, 0.0), axis=1, keepdims=True).astype(jnp.int32)
    owner_hot = jnp.where(iota((ns, T), 0) == own_row, 1.0, 0.0).astype(BF16)
    at_rank = iota((T, 128), 1) == rank_col
    hi = jnp.where(at_rank, (loc_col >> 5).astype(F32), 0.0).astype(BF16)
    lo = jnp.where(at_rank, (loc_col & 31).astype(F32), 0.0).astype(BF16)
    req = mm(owner_hot, hi, ((1,), (0,))) * 32.0 + mm(owner_hot, lo, ((1,), (0,)))
    for s in range(ns):
        req_s[s] = req[s : s + 1, :]
    req_r[me] = req_s[me]

    pl.semaphore_wait(bar, ns - 1 + len(near_z) + len(far_z))

    for gi, dys in enumerate(groups(ny)):
        for dy in dys:

            def send_req(k, c):
                peer = rem(y + ny - dy, ny) * row + rem(me + k, row)
                copy(req_s.at[peer], req_r.at[me], 0, {"table": peer}, rs_req.at[gi])
                return c

            lax.fori_loop(0 if dy else 1, row, send_req, 0)

    for i in (1, 2, 3):
        loads[i].start()

    loads[0].wait()
    loads[6].wait()
    adm = adm_ref[...].astype(F32)
    ones = jnp.ones((R, 128), BF16)
    for gi, dys in enumerate(groups(ny)):
        n = len(dys)
        wait_bytes(req_r.at[pl.ds(0, n * row - (0 in dys))], rs_req.at[gi])
        hot = []
        for dy in dys:
            yy = rem(y + dy, ny)
            r = jnp.broadcast_to(req_r[pl.ds(yy * row, row)], (row, CAP, 128))
            r = jnp.where(iota((row, CAP, 128), 1) == iota((row, CAP, 128), 2), r, 0.0)
            r = jnp.sum(r, axis=2, keepdims=True).reshape(row * CAP, 1).astype(jnp.int32)
            hot.append(jnp.where(iota((row * CAP, R), 1) == r, adm, 0.0).astype(BF16))
        hot = jnp.concatenate(hot, axis=0)
        got = mm(hot, table_v[...], ((1,), (0,)))
        got = jnp.concatenate(
            [got[:, :H].reshape(n * row, CAP, H), got[:, H:].reshape(n * row, CAP, H)], axis=1
        ).astype(BF16)
        for j, dy in enumerate(dys):
            yy = rem(y + dy, ny)
            rows_s[pl.ds(yy * row, row)] = got[j * row : (j + 1) * row]

        for dy in dys:

            def send_rows(k, c):
                peer = rem(y + dy, ny) * row + rem(me + k, row)
                copy(rows_s.at[peer], rows_r.at[me], 1, {"table": peer}, rs_rows.at[gi])
                return c

            lax.fori_loop(0 if dy else 1, row, send_rows, 0)
        flg = mm(hot, ones, ((1,), (0,))).reshape(n * row, CAP, 128)
        flg = jnp.where(iota(flg.shape, 1) == iota(flg.shape, 2), flg, 0.0)
        flg = jnp.sum(flg, axis=1, keepdims=True)
        for j, dy in enumerate(dys):
            yy = rem(y + dy, ny)
            flg_s[pl.ds(yy * row, row)] = flg[j * row : (j + 1) * row]

    def send_flg(k, c):
        peer = rem(me + k, ns)
        copy(flg_s.at[peer], flg_r.at[me], 2, {"table": peer})
        return c

    lax.fori_loop(1, ns, send_flg, 0)
    rows_r[me] = rows_s[me]
    flg_r[me] = flg_s[me]

    slot = own_col * (2 * CAP) + rank_col
    pi = iota((T, ns * 2 * CAP), 1)
    perm[pl.ds(0, T)] = jnp.where(pi == slot, 1.0, 0.0).astype(BF16)
    perm[pl.ds(T, T)] = jnp.where(pi == slot + CAP, 1.0, 0.0).astype(BF16)

    loads[5].wait()
    l0 = len_ref[:, 0:1]
    l1 = l0 + len_ref[:, 1:2]
    l2 = l1 + len_ref[:, 2:3]

    def segment(pos):
        one = jnp.where(pos >= l0, 1, 0)
        two = jnp.where(pos >= l1, 1, 0)
        return one + two + jnp.where(pos >= l2, 1, 0)

    vism[...] = jnp.where((segment(ri) == segment(ci)) & (ci <= ri), 1.0 / MOST, 0.0)

    loads[1].wait()
    loads[2].wait()
    gmix[...] = mm(og_v[...], wout_v[...], ((1,), (1,)))
    loads[3].wait()

    last = len(groups(ny)) - 1
    for gi, dys in enumerate(groups(ny)):
        wait_bytes(rows_r.at[pl.ds(0, len(dys) * row - (0 in dys))], rs_rows.at[gi])
        got = acc[...] if gi else None
        for dy in dys:
            yy = rem(y + ny - dy, ny)
            wide = row * 2 * CAP
            part = mm(
                perm[:, pl.ds(pl.multiple_of(yy * wide, wide), wide)],
                rows_r[pl.ds(yy * row, row)].reshape(wide, H),
                ((1,), (0,)),
            )
            got = part if got is None else got + part
        if gi < last:
            acc[...] = got
    fet = jnp.concatenate([got[:T], got[T:]], axis=1)
    fet_v[...] = fet
    cen = fet - jnp.sum(fet, axis=1, keepdims=True) * (1.0 / D)
    inv = lax.rsqrt(jnp.sum(cen * cen, axis=1, keepdims=True) * (1.0 / D) + EPS)
    nrm = cen * inv
    nrm_f[...] = nrm
    nrm_b[...] = nrm.astype(BF16)

    wide = min(256, 4 * W)
    for n in range(4 * W // wide):
        cols = slice(n * wide, (n + 1) * wide)
        p = mm(nrm_b[...], win_v[:, cols], ((1,), (0,)))
        proj[:, cols] = p
        act[:, cols] = (p * sigmoid(p)).astype(BF16)

    for h in range(HEADS):
        v = act[:, W + h * hd : W + (h + 1) * hd]
        q = act[:, 2 * W + h * hd : 2 * W + (h + 1) * hd]
        k = act[:, 3 * W + h * hd : 3 * W + (h + 1) * hd]
        s = mm(q, k, ((1,), (1,)))
        sco[h] = s
        w = (s * sigmoid(s) * vism[...]).astype(BF16)
        wts[h] = w
        att[:, h * hd : (h + 1) * hd] = mm(w, v, ((1,), (0,)))

    a = att[...]
    a = a - jnp.sum(a, axis=1, keepdims=True) * (1.0 / W)
    hscale = lax.rsqrt(jnp.sum(a * a, axis=1, keepdims=True) * (1.0 / W) + EPS)
    hn = a * hscale
    hnorm[...] = hn
    mix[...] = (hn * act[:, :W].astype(F32)).astype(BF16)

    factor = 1.0 / math.sqrt(T * nz * ns)
    partner = me + 1 - 2 * core
    Q = H // 2
    E = H // 4
    for c in range(2):
        for h in range(2):
            wt = mm(mix[...], og_v[:, h * H + c * Q : h * H + (c + 1) * Q], ((0,), (0,))) * factor
            wt = wt.reshape(ny, NX, 2, 8, Q)
            for xx in range(NX):
                for cc in range(2):
                    wt_f[c, cc, xx, :, h * 8 : (h + 1) * 8, :] = wt[:, xx, cc]
        for i in range(NX):
            xx = rem(x + NX // 2 + i, NX)
            w1_s[c, xx] = wt_f[c, 1 - core, xx].astype(BF16)
            copy(w1_s.at[c, xx], w1_r.at[c, xx], 3, {"table": partner}, rs1.at[c * NX + xx])

    def along_x(xx):
        return {"table": (y * NX + xx) * 2 + core}

    def along_y(src, dst, i):
        def send(k, c):
            yy = rem(y + k, ny)
            copy(src.at[yy], dst.at[y], i, {"table": (yy * NX + x) * 2 + core})
            return c

        lax.fori_loop(1, ny, send, 0)

    for c in range(2):
        for i in range(NX):
            xx = rem(x + NX // 2 + i, NX)
            wait_bytes(w1_r.at[c, xx], rs1.at[c * NX + xx])
            total = wt_f[c, core, xx] + w1_r[c, xx].astype(F32)
            mine = i == NX - NX // 2
            if c == 0:
                xa1_s[xx] = total.astype(BF16)
                if not mine:
                    copy(xa1_s.at[xx], xa1_r.at[x], 4, along_x(xx))
            else:
                xa2_s[xx] = total[..., :E].astype(BF16)
                if not mine:
                    copy(xa2_s.at[xx], xa2_r.at[x], 5, along_x(xx))
                yb_s[:, xx] = total[..., E:].astype(BF16)
    xa1_r[x] = xa1_s[x]
    xa2_r[x] = xa2_s[x]
    along_y(yb_s, yb_r, 6)
    yb_r[y] = yb_s[y]

    lo_v[...] = (fet_v[...] + mm(mix[...], wout_v[...], ((1,), (0,)))).astype(BF16)

    g = gmix[...] * act[:, :W].astype(F32)
    hn = hnorm[...]
    g = g - jnp.sum(g, axis=1, keepdims=True) * (1.0 / W) - hn * (jnp.sum(g * hn, axis=1, keepdims=True) * (1.0 / W))
    gatt[...] = (hscale * g).astype(BF16)

    def through_silu(grad, at):
        p = proj[:, at : at + grad.shape[1]]
        s = sigmoid(p)
        gproj[:, at : at + grad.shape[1]] = (grad * (s * (1.0 + p * (1.0 - s)))).astype(BF16)

    through_silu(gmix[...] * hn, 0)
    for h in range(HEADS):
        v = act[:, W + h * hd : W + (h + 1) * hd]
        q = act[:, 2 * W + h * hd : 2 * W + (h + 1) * hd]
        k = act[:, 3 * W + h * hd : 3 * W + (h + 1) * hd]
        ga = gatt[:, h * hd : (h + 1) * hd]
        gw = mm(ga, v, ((1,), (1,)))
        gv = mm(wts[h], ga, ((0,), (0,)))
        sv = sco[h]
        s = sigmoid(sv)
        gs = (gw * (s * (1.0 + sv * (1.0 - s))) * vism[...]).astype(BF16)
        gq = mm(gs, k, ((1,), (0,)))
        gk = mm(gs, q, ((0,), (0,)))
        through_silu(gv, W + h * hd)
        through_silu(gq, 2 * W + h * hd)
        through_silu(gk, 3 * W + h * hd)

    def add_up(ref, n):
        total = ref[0].astype(F32)
        for i in range(1, n):
            total = total + ref[i].astype(F32)
        return total.astype(BF16)

    wait_bytes(xa1_r.at[pl.ds(0, NX - 1)], rs.at[4])
    ya1_s[...] = add_up(xa1_r, NX)
    along_y(ya1_s, ya1_r, 7)
    ya1_r[y] = ya1_s[y]
    wait_bytes(xa2_r.at[pl.ds(0, NX - 1)], rs.at[5])
    ya2_s[...] = add_up(xa2_r, NX)
    along_y(ya2_s, ya2_r, 8)
    ya2_r[y] = ya2_s[y]
    wait_bytes(yb_r.at[pl.ds(0, ny - 1)], rs.at[6])
    xb_s[...] = add_up(yb_r, ny)
    for i in range(1, NX):
        xx = rem(x + i, NX)
        copy(xb_s.at[xx], xb_r.at[x], 9, along_x(xx))
    xb_r[x] = xb_s[x]

    gn = mm(gproj[...], win_v[...], ((1,), (1,)))
    nrm = nrm_f[...]
    m1 = jnp.sum(gn, axis=1, keepdims=True) * (1.0 / D)
    m2 = jnp.sum(gn * nrm, axis=1, keepdims=True) * (1.0 / D)
    wait_bytes(flg_r.at[pl.ds(0, ns - 1)], rs.at[2])
    flags = jnp.concatenate([flg_r[s] for s in range(ns)], axis=0).astype(BF16)
    own_hot = jnp.where(iota((T, ns), 1) == own_col, 1.0, 0.0).astype(BF16)
    flag = mm(own_hot, flags, ((1,), (0,)))
    flag = jnp.sum(jnp.where(at_rank, flag, 0.0), axis=1, keepdims=True)
    eg_v[...] = flag * (inv * (gn - m1 - nrm * m2) + og_v[...].astype(F32))

    def to_near(ref, i):
        for to in near_z:
            copy(ref.at[zl], ref.at[zl], i, {"dp": to})

    def to_far(ref, src, i):
        if near > 1:
            wait_bytes(src.at[pl.ds(0, near - 1)], rs.at[i])
        ref[zg_me] = add_up(src, near)
        for to in far_z:
            copy(ref.at[zg_me], ref.at[zg_me], i + 2, {"dp": to})

    wait_bytes(ya1_r.at[pl.ds(0, ny - 1)], rs.at[7])
    zr1[zl] = add_up(ya1_r, ny)
    to_near(zr1, 10)
    wait_bytes(ya2_r.at[pl.ds(0, ny - 1)], rs.at[8])
    zr2[zl, :, pl.ds(0, E)] = add_up(ya2_r, ny)
    wait_bytes(xb_r.at[pl.ds(0, NX - 1)], rs.at[9])
    zr2[zl, :, pl.ds(E, E)] = add_up(xb_r, NX)
    to_near(zr2, 11)
    to_far(zg1, zr1, 10)
    to_far(zg2, zr2, 11)
    for c, ref in enumerate((zg1, zg2)):
        if far > 1:
            wait_bytes(ref.at[pl.ds(0, far - 1)], rs.at[12 + c])
        total = ref[0].astype(F32)
        for i in range(1, far):
            total = total + ref[i].astype(F32)
        wg_v[:, c * Q : (c + 1) * Q] = total[:8]
        wg_v[:, H + c * Q : H + (c + 1) * Q] = total[8:]

    wait_bytes(req_s.at[pl.ds(0, ns - 1)], ss.at[0])
    wait_bytes(rows_s.at[pl.ds(0, ns - 1)], ss.at[1])
    wait_bytes(flg_s.at[pl.ds(0, ns - 1)], ss.at[2])
    wait_bytes(w1_s, ss.at[3])
    for i, (ref, n) in enumerate(
        ((xa1_s, NX), (xa2_s, NX), (yb_s, ny), (ya1_s, ny), (ya2_s, ny), (xb_s, NX), (zr1, near), (zr2, near), (zg1, far), (zg2, far))
    ):
        if n > 1:
            wait_bytes(ref.at[pl.ds(0, n - 1)], ss.at[4 + i])


def write_out(lo, eg, wg, lo_out, eg_out, wg_out, sems):
    n = lo.shape[0] // 4
    copies = [(eg.at[pl.ds(i * n, n)], eg_out.at[pl.ds(i * n, n)]) for i in range(4)]
    copies += [(lo.at[pl.ds(i * n * 2, n * 2)], lo_out.at[pl.ds(i * n * 2, n * 2)]) for i in range(2)]
    copies = [pltpu.make_async_copy(a, b, sems.at[i]) for i, (a, b) in enumerate(copies + [(wg, wg_out)])]
    for c in copies:
        c.start()
    for c in copies:
        c.wait()


def on_device(nz, item_ids, lengths, item_table, admitted, input_weight, output_weight, out_grad):
    ns = lax.axis_size("table")
    ny = ns // (2 * NX)
    T = item_ids.shape[0]
    R, D = item_table.shape
    W = output_weight.shape[0]
    H = D // 2
    Q = H // 2
    E = H // 4
    near, far = z_split(nz)
    V = pltpu.VMEM
    vspec = pl.BlockSpec(memory_space=pltpu.VMEM)
    hspec = pl.BlockSpec(memory_space=pltpu.HBM)
    scratch = [
        V((1, T), jnp.int32), V((1, 4), jnp.int32), V((1, R), jnp.int32),
        V((R, D), BF16), V((D, 4 * W), BF16), V((W, D), BF16), V((T, D), BF16),
        V((ns, 1, 128), F32), V((ns, 1, 128), F32), V((ns, 1, 128), F32), V((ns, 1, 128), F32),
        V((ns, 2 * CAP, H), BF16), V((ns, 2 * CAP, H), BF16),
        V((2 * T, ns * 2 * CAP), BF16), V((T, D), F32), V((T, D), F32), V((T, D), BF16),
        V((T, 4 * W), F32), V((T, 4 * W), BF16), V((T, T), F32), V((HEADS, T, T), F32), V((HEADS, T, T), BF16),
        V((T, W), F32), V((T, W), F32), V((T, W), BF16), V((T, W), F32), V((T, W), BF16), V((T, 4 * W), BF16),
        V((2, 2, NX, ny, 16, Q), F32), V((2, NX, ny, 16, Q), BF16), V((2, NX, ny, 16, Q), BF16),
        V((NX, ny, 16, Q), BF16), V((NX, ny, 16, Q), BF16), V((NX, ny, 16, E), BF16), V((NX, ny, 16, E), BF16),
        V((ny, NX, 16, E), BF16), V((ny, NX, 16, E), BF16),
        V((ny, 16, Q), BF16), V((ny, 16, Q), BF16), V((ny, 16, E), BF16), V((ny, 16, E), BF16),
        V((NX, 16, E), BF16), V((NX, 16, E), BF16),
        V((near, 16, Q), BF16), V((near, 16, Q), BF16), V((far, 16, Q), BF16), V((far, 16, Q), BF16),
        V((2 * T, H), F32),
        pltpu.SemaphoreType.DMA((7,)),
        pltpu.SemaphoreType.DMA((14,)), pltpu.SemaphoreType.DMA((14,)),
        pltpu.SemaphoreType.DMA((len(groups(ny)),)), pltpu.SemaphoreType.DMA((len(groups(ny)),)), pltpu.SemaphoreType.DMA((2 * NX,)),
    ]
    results = pl.pallas_call(
        functools.partial(kernel, nz, ns),
        out_shape=(V((T, D), BF16), V((T, D), F32), V((8, D), F32)),
        in_specs=[hspec] * 7,
        out_specs=(vspec, vspec, vspec),
        scratch_shapes=scratch,
        compiler_params=pltpu.CompilerParams(
            collective_id=0, has_side_effects=True, vmem_limit_bytes=60 * 1024 * 1024
        ),
        name="layer",
    )(
        item_ids.reshape(1, T), lengths, admitted.reshape(1, R), item_table, input_weight, output_weight, out_grad
    )
    return pl.pallas_call(
        write_out,
        out_shape=(
            jax.ShapeDtypeStruct((T, D), BF16),
            jax.ShapeDtypeStruct((T, D), F32),
            jax.ShapeDtypeStruct((8, D), F32),
        ),
        in_specs=[vspec] * 3,
        out_specs=(hspec,) * 3,
        scratch_shapes=[pltpu.SemaphoreType.DMA((7,))],
        compiler_params=pltpu.CompilerParams(vmem_limit_bytes=16 * 1024 * 1024),
        name="write_out",
    )(*results)


def solution(mesh):
    return jax.shard_map(
        functools.partial(on_device, mesh.shape["dp"]),
        mesh=mesh,
        in_specs=(
            P(("dp", "table")),
            P(("dp", "table"), None),
            P("table", None),
            P("table"),
            P(),
            P(),
            P(("dp", "table"), None),
        ),
        out_specs=(P(("dp", "table"), None), P(("dp", "table"), None), P("table", None)),
        check_vma=False,
    )
```

time: 78.6 us -> 77.3 us (0.983)
  Pallas kernels: 77.8 us -> 76.5 us
    pallas_call x1, Pallas kernels: 76.6 us -> 75.3 us  [on_device(): pl.pallas_call(functools.partial(kernel, nz, ns), out_shape=(V((T, D), BF...]
where the time goes in v3:
time: 77.3 us; the launch traced here: 77.1 us
  Pallas kernels  76.5 us (99%)
    pallas_call x1, Pallas kernels, on_device(): pl.pallas_call(functools.partial(kernel, nz, ns), out_shape=(V((T, D), BF...  75.3 us

profile of v3, /device:TPU:8, one launch (start us, length us, event | category | flops | bytes accessed | tf_op | source)
XLA Modules:
  0.0 77.1 jit_solution(5421491375370121852)
XLA Ops:
  0.6 75.3 %layer.1 = (bf16[256,1024]{1,0:T(8,128)(2,1)S(1)}, f32[256,1024]{1,0:T(8,128)S(1)}, f32[8,1024]{1,0:T(8,128)S(1)}) custom-call(s32[1,256]{1,0:T(1,128)} %bitcast.3, s32[1,4]{1,0:T(1,128)} %len_hbm.1, s32[1,1024]{1,0:T(1,128)} %bitcast.2, bf16[1024,1024]{1,0:T(8,128)(2,1)} %table_hbm.1, bf16[1024,2048]{1,0:T(8,128)(2,1)} %win_hbm.1, ...), custom_call_target="tpu_custom_call" | custom-call | tf_op jit(solution)/shard_map/layer/pallas_call | solution.py:452
  75.9 1.2 %write_out.1 = (bf16[256,1024]{1,0:T(8,128)(2,1)}, f32[256,1024]{1,0:T(8,128)}, f32[8,1024]{1,0:T(8,128)}) custom-call(bf16[256,1024]{1,0:T(8,128)(2,1)S(1)} %get-tuple-element.6.lo, f32[256,1024]{1,0:T(8,128)S(1)} %get-tuple-element.7.eg, f32[8,1024]{1,0:T(8,128)S(1)} %get-tuple-element.8.wg), custom_call_target="tpu_custom_call" | custom-call | tf_op jit(solution)/shard_map/write_out/pallas_call | solution.py:465

commit v4 on v3

--- a/solution.py
+++ b/solution.py
@@ -233,8 +233,9 @@
     nrm_f[...] = nrm
     nrm_b[...] = nrm.astype(BF16)
 
-    wide = min(256, 4 * W)
-    for n in range(4 * W // wide):
+    wide = min(256, W)
+    first = W // wide
+    for n in list(range(first, 4 * first)) + list(range(first)):
         cols = slice(n * wide, (n + 1) * wide)
         p = mm(nrm_b[...], win_v[:, cols], ((1,), (0,)))
         proj[:, cols] = p

time: 77.3 us -> 77.2 us (level)
  no operation moved by 1% of the time
where the time goes in v4:
time: 77.2 us; the launch traced here: 77 us
  Pallas kernels  76.4 us (99%)
    pallas_call x1, Pallas kernels, on_device(): pl.pallas_call(functools.partial(kernel, nz, ns), out_shape=(V((T, D), BF...  75.2 us

profile of v4, /device:TPU:8, one launch (start us, length us, event | category | flops | bytes accessed | tf_op | source)
XLA Modules:
  0.0 77.0 jit_solution(6252136263218130263)
XLA Ops:
  0.6 75.2 %layer.1 = (bf16[256,1024]{1,0:T(8,128)(2,1)S(1)}, f32[256,1024]{1,0:T(8,128)S(1)}, f32[8,1024]{1,0:T(8,128)S(1)}) custom-call(s32[1,256]{1,0:T(1,128)} %bitcast.3, s32[1,4]{1,0:T(1,128)} %len_hbm.1, s32[1,1024]{1,0:T(1,128)} %bitcast.2, bf16[1024,1024]{1,0:T(8,128)(2,1)} %table_hbm.1, bf16[1024,2048]{1,0:T(8,128)(2,1)} %win_hbm.1, ...), custom_call_target="tpu_custom_call" | custom-call | tf_op jit(solution)/shard_map/layer/pallas_call | solution.py:453
  75.8 1.2 %write_out.1 = (bf16[256,1024]{1,0:T(8,128)(2,1)}, f32[256,1024]{1,0:T(8,128)}, f32[8,1024]{1,0:T(8,128)}) custom-call(bf16[256,1024]{1,0:T(8,128)(2,1)S(1)} %get-tuple-element.6.lo, f32[256,1024]{1,0:T(8,128)S(1)} %get-tuple-element.7.eg, f32[8,1024]{1,0:T(8,128)S(1)} %get-tuple-element.8.wg), custom_call_target="tpu_custom_call" | custom-call | tf_op jit(solution)/shard_map/write_out/pallas_call | solution.py:466
